TPU v7x, 32 devices: a whole 2x2x4 slice. The times are simulated.
32 devices in a mesh: groups: 2 (over x), goal: 16 (over z, y, core).
Axes of the slice: x: 2, y: 2, z: 4, core: 2. Of those that a mesh axis runs over, the one named last changes fastest.
Arguments:
- queries: bfloat16 [128, 64, 4096], P(('groups', 'goal')), parts along dimension 0, may hold values from -8 to 8
- goal_keys: bfloat16 [32, 256, 4096], P(('groups', 'goal')), parts along dimension 0, may hold values from -8 to 8
- goal_values: bfloat16 [32, 256, 4096], P(('groups', 'goal')), parts along dimension 0, may hold values from -6 to 6
- out_weight: bfloat16 [4096, 2048], P('goal'), may hold values from -0.5 to 0.5
- tactic_goal: int32 [128, 1], P(('groups', 'goal')), parts along dimension 0, may hold values from 0 to 15
- tactic_len: int32 [128], P(('groups', 'goal')), parts along dimension 0, may hold values from 1 to 64
Outputs:
- projected: bfloat16 [128, 64, 2048], P(('groups', 'goal')), parts along dimension 0
There are 2 independent parts, one for each index of `groups`. A program takes and returns all parts, laid end to end along the dimension named above; an argument that names none is the same for every part. Nothing has to cross between parts.
Inputs may be any that keep to these rules, and one draw needn't show every extreme that they name: `tactic_goal`: every goal is read by at least one tactic; tactics per goal are uneven. `tactic_len`: the live positions of a tactic are its leading ones.
All inputs are finite; a program needn't handle non-finite values.
Results may differ from a plain program's by a relative error of at most 0.01.
Values may be sent and summed in bfloat16 or wider, within the bound.
A program may use at most 192 MiB of HBM per device.

v0:
```python
import math
import jax
import jax.numpy as jnp
from jax import lax
from jax.sharding import PartitionSpec as P

DH = 64


def attend_block(query_block, keys_heads, values_heads, block_ids):
    tact_count = query_block.shape[0]
    row_count = query_block.shape[1]
    width_local = query_block.shape[2]
    head_count = width_local // DH
    keys_tact = jnp.take(keys_heads, block_ids, axis=0).reshape(tact_count, -1, head_count, DH)
    vals_tact = jnp.take(values_heads, block_ids, axis=0).reshape(tact_count, -1, head_count, DH)
    query_four = query_block.reshape(tact_count, row_count, head_count, DH)
    scores = jnp.einsum(
        "tihd,tjhd->thij", query_four, keys_tact, preferred_element_type=jnp.float32
    )
    biggest = jnp.max(scores, axis=-1, keepdims=True)
    powers = jnp.exp(scores - biggest)
    weights = (powers / jnp.sum(powers, axis=-1, keepdims=True)).astype(jnp.bfloat16)
    attended = jnp.einsum("thij,tjhd->tihd", weights, vals_tact, preferred_element_type=jnp.float32)
    return attended.reshape(tact_count, row_count, width_local).astype(jnp.bfloat16)


def attend(query_piece, keys_heads, values_heads, goal_ids):
    tact_count = query_piece.shape[0]
    row_count = query_piece.shape[1]
    width_local = query_piece.shape[2]
    block_size = math.gcd(tact_count, 64)
    block_count = tact_count // block_size
    query_blocks = query_piece.reshape(block_count, block_size, row_count, width_local)
    id_blocks = goal_ids.reshape(block_count, block_size)

    def one_block(operands):
        return attend_block(operands[0], keys_heads, values_heads, operands[1])

    results = lax.map(one_block, (query_blocks, id_blocks))
    return results.reshape(tact_count, row_count, width_local)


def shards(queries, goal_keys, goal_values, out_weight, tactic_goal, tactic_len):
    goal_ids = lax.all_gather(tactic_goal[:, 0], "goal", axis=0, tiled=True)
    keys_heads, values_heads = (
        lax.all_to_all(goal_keys, "goal", split_axis=2, concat_axis=0, tiled=True),
        lax.all_to_all(goal_values, "goal", split_axis=2, concat_axis=0, tiled=True),
    )
    query_heads = lax.all_to_all(queries, "goal", split_axis=2, concat_axis=0, tiled=True)
    attended = attend(query_heads, keys_heads, values_heads, goal_ids)
    merged = lax.all_to_all(attended, "goal", split_axis=0, concat_axis=2, tiled=True)
    live_rows = jnp.arange(merged.shape[1])[None, :] < tactic_len[:, None]
    context = jnp.where(live_rows[:, :, None], merged, jnp.zeros_like(merged))
    tact_local = context.shape[0]
    row_count = context.shape[1]
    flat = context.reshape(tact_local * row_count, context.shape[2])
    projected = jnp.dot(
        flat,
        lax.all_gather(out_weight, "goal", axis=0, tiled=True),
        preferred_element_type=jnp.float32,
    )
    return projected.astype(jnp.bfloat16).reshape(tact_local, row_count, out_weight.shape[1])


def solution(mesh):
    return jax.shard_map(
        shards,
        mesh=mesh,
        in_specs=(
            P(("groups", "goal"), None, None),
            P(("groups", "goal"), None, None),
            P(("groups", "goal"), None, None),
            P("goal", None),
            P(("groups", "goal"), None),
            P(("groups", "goal")),
        ),
        out_specs=P(("groups", "goal"), None, None),
        check_vma=False,
    )
```

profile of v0, /device:TPU:13, one launch (start us, length us, event | category | flops | bytes accessed | tf_op | source)
XLA Modules:
  0.0 509.1 jit_solution(2314349538631211243)
XLA Ops:
  7.3 10.1 %copy.23 = bf16[1,256,4096]{1,0,2:T(2,128)(2,1)} copy(bf16[1,256,4096]{2,1,0:T(8,128)(2,1)} %param.10) | data formatting | bytes 4194304 | tf_op args[2]
  17.8 21.7 %reduce.1 = bf16[4096,256]{1,0:T(8,128)(2,1)S(1)} reduce(bf16[4096,1,256]{2,1,0:T(2,128)(2,1)} %bitcast.58, bf16[]{:T(256)} %broadcast.32), dimensions={1}, to_apply=%bitcast.44.reduce_sub_computation | reduce | bytes 4194306
  41.6 6.6 %all-to-all-start = ((bf16[16,2,32768]{2,1,0:T(2,128)(2,1)}), bf16[16,2,32768]{2,1,0:T(2,128)(2,1)S(1)}, u32[]{:S(2)}, u32[]{:S(2)}) async-start(bf16[16,2,32768]{2,1,0:T(2,128)(2,1)} %reshape.91), calls=%async_computation | async-start | bytes 4194304 | tf_op jit(solution)/shard_map/all_to_all | solution.py:48
  48.1 10.1 %copy.26 = bf16[1,256,4096]{1,0,2:T(2,128)(2,1)} copy(bf16[1,256,4096]{2,1,0:T(8,128)(2,1)} %param.9) | data formatting | bytes 4194304 | tf_op args[1]
  58.2 23.0 %reduce = bf16[4096,256]{1,0:T(8,128)(2,1)} reduce(bf16[4096,1,256]{2,1,0:T(2,128)(2,1)} %bitcast.59, bf16[]{:T(256)} %broadcast.32), dimensions={1}, to_apply=%bitcast.46.reduce_sub_computation | reduce | bytes 4194306
  81.1 4.0 reshape.93
  85.1 58.2 %all-to-all-done = bf16[16,2,32768]{2,1,0:T(2,128)(2,1)S(1)} async-done(((bf16[16,2,32768]{2,1,0:T(2,128)(2,1)}), bf16[16,2,32768]{2,1,0:T(2,128)(2,1)S(1)}, u32[]{:S(2)}, u32[]{:S(2)}) %all-to-all-start) | async-done | bytes 2097184 | tf_op jit(solution)/shard_map/all_to_all | solution.py:48
  143.3 4.3 all-to-all-start.1
  147.7 7.0 %copy.29 = bf16[4,64,4096]{1,0,2:T(4,128)(2,1)} copy(bf16[4,64,4096]{2,1,0:T(8,128)(2,1)} %param.8) | data formatting | bytes 4194304 | tf_op args[0]
  154.7 7.5 %reshape.95 = bf16[16,2,32768]{2,1,0:T(2,128)(2,1)} reshape(bf16[4096,4,64]{2,1,0:T(4,128)(2,1)} %bitcast.63) | data formatting | bytes 4194304
  162.3 52.0 %all-to-all-done.1 = bf16[16,2,32768]{2,1,0:T(2,128)(2,1)} async-done(((bf16[16,2,32768]{2,1,0:T(2,128)(2,1)}), bf16[16,2,32768]{2,1,0:T(2,128)(2,1)}, u32[]{:S(2)}, u32[]{:S(2)}) %all-to-all-start.1) | async-done | bytes 2097184 | tf_op jit(solution)/shard_map/all_to_all | solution.py:47
  214.3 4.7 all-to-all-start.2
  220.4 44.1 %all-reduce = s32[64]{0:T(128)S(1)} all-reduce(s32[64]{0:T(128)S(1)} %bitcast_dynamic-update-slice_fusion), channel_id=2, replica_groups=mesh['groups'=2,'goal'=16] {'goal'}, use_global_device_ids=true, to_apply=%add | all-reduce | flops 64 | bytes 512 | tf_op jit(solution)/shard_map/all_gather | solution.py:45
  264.5 6.8 %reshape.92 = bf16[4096,1,256]{2,1,0:T(2,128)(2,1)} reshape(bf16[16,2,32768]{2,1,0:T(2,128)(2,1)S(1)} %all-to-all-done) | data formatting | bytes 4194304
  271.3 3.9 copy.34
  278.0 10.5 %reshape.94 = bf16[4096,1,256]{2,1,0:T(2,128)(2,1)} reshape(bf16[16,2,32768]{2,1,0:T(2,128)(2,1)} %all-to-all-done.1) | data formatting | bytes 4194304
  288.5 3.9 copy.35
  292.4 3.9 copy.27
  296.3 5.5 %gather_fusion = bf16[64,256,256]{2,1,0:T(8,128)(2,1)} fusion(bf16[16,256,256]{2,1,0:T(8,128)(2,1)S(1)} %bitcast.56, s32[1024]{0:T(1024)S(1)} %pad_clamp_fusion), kind=kCustom, calls=%fused_computation.clone | custom fusion | bytes 16777472 | tf_op jit(solution)/shard_map/while/body/eval_jaxpr/jit(_take)/gather | solution.py:16
  301.8 7.1 %gather_fusion.1 = bf16[64,256,256]{2,1,0:T(8,128)(2,1)} fusion(bf16[16,256,256]{2,1,0:T(8,128)(2,1)} %bitcast.57, s32[1024]{0:T(1024)S(1)} %pad_clamp_fusion), kind=kCustom, calls=%fused_computation.1.clone | custom fusion | bytes 16777472 | tf_op jit(solution)/shard_map/while/body/eval_jaxpr/jit(_take)/gather | solution.py:15
  308.9 11.6 %broadcast_select_fusion = (bf16[64,256,256]{2,1,0:T(8,128)(2,1)}, bf16[64,256,256]{2,1,0:T(8,128)(2,1)}) fusion(bf16[64,256,256]{2,1,0:T(8,128)(2,1)} %gather_fusion.1, pred[64]{0:T(512)(128)(4,1)S(1)} %compare_and_fusion, bf16[64,256,256]{2,1,0:T(8,128)(2,1)} %gather_fusion), kind=kLoop, calls=%fused_computation.9 | loop fusion | flops 8388608 | bytes 33554496 | tf_op jit(solution)/shard_map/while/body/eval_jaxpr/jit(_take)/select_n | solution.py:15
  320.5 11.9 %copy.28 = bf16[64,256,256]{1,2,0:T(8,128)(2,1)} copy(bf16[64,256,256]{2,1,0:T(8,128)(2,1)} %get-tuple-element.16) | data formatting | bytes 16777216 | tf_op jit(solution)/shard_map/while/body/eval_jaxpr/jit(_take)/select_n | solution.py:15
  332.4 7.5 %reshape.96 = bf16[4096,4,64]{2,1,0:T(4,128)(2,1)} reshape(bf16[16,2,32768]{2,1,0:T(2,128)(2,1)} %all-to-all-done.2) | data formatting | bytes 4194304
  339.9 5.4 %copy.30 = bf16[4,64,16,256]{3,1,0,2:T(8,128)(2,1)S(1)} copy(bf16[4,64,16,256]{1,0,3,2:T(4,128)(2,1)} %bitcast.62) | data formatting | bytes 4194304 | tf_op jit(solution)/shard_map/all_to_all | solution.py:50
  348.5 11.9 %copy.25 = bf16[64,256,256]{1,2,0:T(8,128)(2,1)} copy(bf16[64,256,256]{2,1,0:T(8,128)(2,1)} %get-tuple-element.17) | data formatting | bytes 16777216 | tf_op jit(solution)/shard_map/while/body/eval_jaxpr/jit(_take)/select_n | solution.py:16
  360.4 12.7 %fusion.6 = f32[64,4,256,64]{2,3,1,0:T(8,128)} fusion(bf16[64,256,4,64]{1,3,2,0:T(8,128)(2,1)} %bitcast.55, bf16[64,64,4,64]{3,2,1,0:T(4,128)(2,1)} %reshape.60), kind=kOutput, calls=%fused_computation.11 | convolution fusion | flops 536870912 | bytes 27262976 | tf_op jit(solution)/shard_map/while/body/eval_jaxpr/tihd,tjhd->thij/dot_general | solution.py:18
  373.1 14.6 %fusion.18 = f32[64,4,64]{2,1,0:T(4,128)S(1)} fusion(f32[64,4,256,64]{2,3,1,0:T(8,128)} %fusion.6), kind=kOutput, calls=%fused_computation.25 | output fusion | flops 8388863 | bytes 16842752 | tf_op jit(solution)/shard_map/while/body/eval_jaxpr/sub | solution.py:22
  387.7 43.3 %fusion.8 = bf16[64,4,64,64]{3,2,1,0:T(8,128)(2,1)} fusion(bf16[64,256,4,64]{1,3,2,0:T(8,128)(2,1)} %bitcast.67, f32[64,4,64]{2,1,0:T(4,128)S(1)} %fusion.18, f32[64,4,256,64]{2,3,1,0:T(8,128)} %fusion.6), kind=kOutput, calls=%fused_computation.13 | convolution fusion | flops 550519040 | bytes 27328512 | tf_op jit(solution)/shard_map/while/body/eval_jaxpr/thij,tjhd->tihd/dot_general | solution.py:24
  431.1 4.8 copy.32
  435.9 7.5 %all-to-all-start.3 = ((bf16[64,64,256]{2,1,0:T(8,128)(2,1)}), bf16[64,64,256]{2,1,0:T(8,128)(2,1)S(1)}, u32[]{:S(2)}, u32[]{:S(2)}) async-start(bf16[64,64,256]{2,1,0:T(8,128)(2,1)} %copy.32), calls=%async_computation.3 | async-start | bytes 4194304 | tf_op jit(solution)/shard_map/all_to_all | solution.py:52
  443.6 47.3 %all-to-all-done.3 = bf16[64,64,256]{2,1,0:T(8,128)(2,1)S(1)} async-done(((bf16[64,64,256]{2,1,0:T(8,128)(2,1)}), bf16[64,64,256]{2,1,0:T(8,128)(2,1)S(1)}, u32[]{:S(2)}, u32[]{:S(2)}) %all-to-all-start.3) | async-done | bytes 2097184 | tf_op jit(solution)/shard_map/all_to_all | solution.py:52
  493.0 9.3 %convolution_convert_fusion = bf16[256,2048]{1,0:T(8,128)(2,1)} fusion(bf16[4096,2048]{1,0:T(8,128)(2,1)} %all-gather.3.cloned.1.call-done, bf16[256,4096]{1,0:T(8,128)(2,1)S(1)} %bitcast.71, pred[256]{0:T(512)(128)(4,1)S(1)} %lt.30), kind=kOutput, calls=%fused_computation.14 | convolution fusion | flops 4296540160 | bytes 19923200 | tf_op jit(solution)/shard_map/dot_general | solution.py:58
  (24 shorter events, 12.4 us)
Async XLA Ops:
  6.5 486.4 %all-gather.3.cloned.1.call-start = ((), (), s32[]{:S(2)}) async-start(), calls=%async_computation.4 | async-start | bytes 17825792 | tf_op jit(solution)/shard_map/all_gather | solution.py:60
  41.6 101.8 %all-to-all-start = ((bf16[16,2,32768]{2,1,0:T(2,128)(2,1)}), bf16[16,2,32768]{2,1,0:T(2,128)(2,1)S(1)}, u32[]{:S(2)}, u32[]{:S(2)}) async-start(bf16[16,2,32768]{2,1,0:T(2,128)(2,1)} %reshape.91), calls=%async_computation | async-start | bytes 4194304 | tf_op jit(solution)/shard_map/all_to_all | solution.py:48
  143.3 71.0 %all-to-all-start.1 = ((bf16[16,2,32768]{2,1,0:T(2,128)(2,1)}), bf16[16,2,32768]{2,1,0:T(2,128)(2,1)}, u32[]{:S(2)}, u32[]{:S(2)}) async-start(bf16[16,2,32768]{2,1,0:T(2,128)(2,1)} %reshape.93), calls=%async_computation.1 | async-start | bytes 4194304 | tf_op jit(solution)/shard_map/all_to_all | solution.py:47
  147.7 71.4 %copy-start.2 = (u32[32]{0:T(128)S(1)}, u32[32]{0:T(128)}, u32[]{:S(2)}) copy-start(u32[32]{0:T(128)} %constant.37) | copy-start | bytes 388
  147.7 72.6 %copy-start = (s32[4,1]{0,1:T(1,128)S(1)}, s32[4,1]{0,1:T(1,128)}, u32[]{:S(2)}) copy-start(s32[4,1]{0,1:T(1,128)} %param.12) | copy-start | bytes 52
  214.3 118.2 %all-to-all-start.2 = ((bf16[16,2,32768]{2,1,0:T(2,128)(2,1)}), bf16[16,2,32768]{2,1,0:T(2,128)(2,1)}, u32[]{:S(2)}, u32[]{:S(2)}) async-start(bf16[16,2,32768]{2,1,0:T(2,128)(2,1)} %reshape.95), calls=%async_computation.2 | async-start | bytes 4194304 | tf_op jit(solution)/shard_map/all_to_all | solution.py:50
  431.1 12.3 %copy-start.1 = (s32[4]{0:T(128)S(1)}, s32[4]{0:T(128)}, u32[]{:S(2)}) copy-start(s32[4]{0:T(128)} %param.13) | copy-start | bytes 52
  435.9 54.9 %all-to-all-start.3 = ((bf16[64,64,256]{2,1,0:T(8,128)(2,1)}), bf16[64,64,256]{2,1,0:T(8,128)(2,1)S(1)}, u32[]{:S(2)}, u32[]{:S(2)}) async-start(bf16[64,64,256]{2,1,0:T(8,128)(2,1)} %copy.32), calls=%async_computation.3 | async-start | bytes 4194304 | tf_op jit(solution)/shard_map/all_to_all | solution.py:52
Sparse Core Ops, SparseCore 0:
  9.5 193.1 all-gather.2
where the time goes:
time: 512 us; the launch traced here: 509 us
  waiting for transfers between devices  158 us (31%)
  local copies, waits for them, and re-layouts  133 us (26%)
  other arithmetic  70.9 us (14%)
  matrix products  65.3 us (13%)
  blocking collectives  44.1 us (9%)
  starting transfers between devices  23.2 us (5%)
  between operations  14.2 us (3%)
    unnamed x22, local copies, waits for them, and re-layouts  75.4 us
    all_to_all x1, waiting for transfers between devices, shards(): lax.all_to_all(goal_values, 'goal', split_axis=2, concat_axis=0, tiled=True)  58.2 us
    all_to_all x1, waiting for transfers between devices, shards(): lax.all_to_all(goal_keys, 'goal', split_axis=2, concat_axis=0, tiled=True)  52 us
    all_to_all x1, waiting for transfers between devices, shards(): lax.all_to_all(attended, 'goal', split_axis=0, concat_axis=2, tiled=True)  47.3 us
    unnamed x2, other arithmetic  44.6 us
    all_gather x1, blocking collectives, shards(): goal_ids = lax.all_gather(tactic_goal[:, 0], 'goal', axis=0, tiled=True)  44.1 us
    dot_general x1, matrix products, attend_block(): jnp.einsum('thij,tjhd->tihd', weights, vals_tact, preferred_element_type=...  43.3 us
    sub x1, other arithmetic, attend_block(): powers = jnp.exp(scores - biggest)  14.6 us
  transfers between devices with their start and end apart: 5, of which 3 were waited for; matrix products, arithmetic and copies ran while one was open for 51% of the time, Pallas kernels for 0%

commit v1 on v0

--- a/solution.py
+++ b/solution.py
@@ -44,7 +44,12 @@
 def shards(queries, goal_keys, goal_values, out_weight, tactic_goal, tactic_len):
     goal_ids = lax.all_gather(tactic_goal[:, 0], "goal", axis=0, tiled=True)
     keys_heads, values_heads = (
-        lax.all_to_all(goal_keys, "goal", split_axis=2, concat_axis=0, tiled=True),
+        jnp.concatenate(
+            lax.all_to_all(
+                jnp.stack(jnp.split(goal_keys, lax.axis_size("goal"), axis=2)), "goal", 0, 0
+            ),
+            axis=0,
+        ),
         lax.all_to_all(goal_values, "goal", split_axis=2, concat_axis=0, tiled=True),
     )
     query_heads = lax.all_to_all(queries, "goal", split_axis=2, concat_axis=0, tiled=True)

time: 512 us -> 493 us (0.963)
  other arithmetic: 70.9 us -> 49.1 us
  waiting for transfers between devices: 158 us -> 172 us
  local copies, waits for them, and re-layouts: 133 us -> 123 us
    all_to_all x1, waiting for transfers between devices: 58.2 us -> 80.7 us  [shards(): lax.all_to_all(goal_values, 'goal', split_axis=2, concat_axis=0, tiled=True)]
    unnamed x2 -> x1, other arithmetic: 44.6 us -> 22.9 us
    all_to_all x1, waiting for transfers between devices: 52 us -> 43.2 us  [shards(): lax.all_to_all(jnp.stack(jnp.split(goal_keys, lax.axis_size('goal'), axis...]
    unnamed x22 -> x35, local copies, waits for them, and re-layouts: 75.4 us -> 66.9 us
  transfers between devices with their start and end apart: 5 -> 5, of which waited for: 3 -> 3; matrix products, arithmetic and copies ran while one was open for 51% -> 46% of each run, Pallas kernels for 0% -> 0%
where the time goes in v1:
time: 493 us; the launch traced here: 490 us
  waiting for transfers between devices  172 us (35%)
  local copies, waits for them, and re-layouts  123 us (25%)
  matrix products  65.2 us (13%)
  other arithmetic  49.1 us (10%)
  blocking collectives  44.1 us (9%)
  starting transfers between devices  23.2 us (5%)
  between operations  14.1 us (3%)
    all_to_all x1, waiting for transfers between devices, shards(): lax.all_to_all(goal_values, 'goal', split_axis=2, concat_axis=0, tiled=True)  80.7 us
    unnamed x35, local copies, waits for them, and re-layouts  66.9 us
    all_to_all x1, waiting for transfers between devices, shards(): lax.all_to_all(attended, 'goal', split_axis=0, concat_axis=2, tiled=True)  47.3 us
    all_gather x1, blocking collectives, shards(): goal_ids = lax.all_gather(tactic_goal[:, 0], 'goal', axis=0, tiled=True)  44.1 us
    all_to_all x1, waiting for transfers between devices, shards(): lax.all_to_all(jnp.stack(jnp.split(goal_keys, lax.axis_size('goal'), axis...  43.2 us
    dot_general x1, matrix products, attend_block(): jnp.einsum('thij,tjhd->tihd', weights, vals_tact, preferred_element_type=...  43.2 us
    unnamed x1, other arithmetic  22.9 us
    sub x1, other arithmetic, attend_block(): powers = jnp.exp(scores - biggest)  14.5 us
  transfers between devices with their start and end apart: 5, of which 3 were waited for; matrix products, arithmetic and copies ran while one was open for 46% of the time, Pallas kernels for 0%

profile of v1, /device:TPU:13, one launch (start us, length us, event | category | flops | bytes accessed | tf_op | source)
XLA Modules:
  0.0 490.3 jit_solution(16885261915778038758)
XLA Ops:
  7.3 1.6 bitcast_dynamic-update-slice_fusion.15
  8.8 1.6 bitcast_dynamic-update-slice_fusion.14
  13.5 1.6 bitcast_dynamic-update-slice_fusion.11
  22.4 6.6 %all-to-all-start.1 = ((bf16[16,1,256,256]{3,2,1,0:T(8,128)(2,1)}), bf16[16,1,256,256]{3,2,1,0:T(8,128)(2,1)S(1)}, u32[]{:S(2)}, u32[]{:S(2)}) async-start(bf16[16,1,256,256]{3,2,1,0:T(8,128)(2,1)} %bitcast_dynamic-update-slice_fusion), calls=%async_computation.1 | async-start | bytes 4194304 | tf_op jit(solution)/shard_map/all_to_all | solution.py:48
  29.0 10.1 %copy.20 = bf16[1,256,4096]{1,0,2:T(2,128)(2,1)} copy(bf16[1,256,4096]{2,1,0:T(8,128)(2,1)} %param.10) | data formatting | bytes 4194304 | tf_op args[2]
  39.5 22.9 %reduce = bf16[4096,256]{1,0:T(8,128)(2,1)} reduce(bf16[4096,1,256]{2,1,0:T(2,128)(2,1)} %bitcast.85, bf16[]{:T(256)} %broadcast.32), dimensions={1}, to_apply=%bitcast.73.reduce_sub_computation | reduce | bytes 4194306
  62.5 4.0 reshape.95
  66.4 43.2 %all-to-all-done.1 = bf16[16,1,256,256]{3,2,1,0:T(8,128)(2,1)S(1)} async-done(((bf16[16,1,256,256]{3,2,1,0:T(8,128)(2,1)}), bf16[16,1,256,256]{3,2,1,0:T(8,128)(2,1)S(1)}, u32[]{:S(2)}, u32[]{:S(2)}) %all-to-all-start.1) | async-done | bytes 2097184 | tf_op jit(solution)/shard_map/all_to_all | solution.py:48
  109.6 4.3 all-to-all-start
  114.0 6.9 %copy.24 = bf16[4,64,4096]{1,0,2:T(4,128)(2,1)} copy(bf16[4,64,4096]{2,1,0:T(8,128)(2,1)} %param.8) | data formatting | bytes 4194304 | tf_op args[0]
  120.9 7.5 %reshape.97 = bf16[16,2,32768]{2,1,0:T(2,128)(2,1)} reshape(bf16[4096,4,64]{2,1,0:T(4,128)(2,1)} %bitcast.88) | data formatting | bytes 4194304
  128.4 80.7 %all-to-all-done = bf16[16,2,32768]{2,1,0:T(2,128)(2,1)} async-done(((bf16[16,2,32768]{2,1,0:T(2,128)(2,1)}), bf16[16,2,32768]{2,1,0:T(2,128)(2,1)}, u32[]{:S(2)}, u32[]{:S(2)}) %all-to-all-start) | async-done | bytes 2097184 | tf_op jit(solution)/shard_map/all_to_all | solution.py:53
  209.1 4.7 all-to-all-start.2
  215.2 44.1 %all-reduce = s32[64]{0:T(128)S(1)} all-reduce(s32[64]{0:T(128)S(1)} %bitcast_dynamic-update-slice_fusion.16), channel_id=2, replica_groups=mesh['groups'=2,'goal'=16] {'goal'}, use_global_device_ids=true, to_apply=%add | all-reduce | flops 64 | bytes 512 | tf_op jit(solution)/shard_map/all_gather | solution.py:45
  259.3 10.4 %reshape.96 = bf16[4096,1,256]{2,1,0:T(2,128)(2,1)} reshape(bf16[16,2,32768]{2,1,0:T(2,128)(2,1)} %all-to-all-done) | data formatting | bytes 4194304
  269.7 3.9 copy.29
  273.6 3.9 copy.21
  277.5 5.5 %gather_fusion.1 = bf16[64,256,256]{2,1,0:T(8,128)(2,1)} fusion(bf16[16,256,256]{2,1,0:T(8,128)(2,1)S(1)} %bitcast.83, s32[1024]{0:T(1024)S(1)} %pad_clamp_fusion), kind=kCustom, calls=%fused_computation.1.clone | custom fusion | bytes 16777472 | tf_op jit(solution)/shard_map/while/body/eval_jaxpr/jit(_take)/gather | solution.py:15
  283.0 7.1 %gather_fusion = bf16[64,256,256]{2,1,0:T(8,128)(2,1)} fusion(bf16[16,256,256]{2,1,0:T(8,128)(2,1)} %bitcast.84, s32[1024]{0:T(1024)S(1)} %pad_clamp_fusion), kind=kCustom, calls=%fused_computation.clone | custom fusion | bytes 16777472 | tf_op jit(solution)/shard_map/while/body/eval_jaxpr/jit(_take)/gather | solution.py:16
  290.1 11.6 %broadcast_select_fusion = (bf16[64,256,256]{2,1,0:T(8,128)(2,1)}, bf16[64,256,256]{2,1,0:T(8,128)(2,1)}) fusion(bf16[64,256,256]{2,1,0:T(8,128)(2,1)} %gather_fusion.1, pred[64]{0:T(512)(128)(4,1)S(1)} %compare_and_fusion, bf16[64,256,256]{2,1,0:T(8,128)(2,1)} %gather_fusion), kind=kLoop, calls=%fused_computation.9 | loop fusion | flops 8388608 | bytes 33554496 | tf_op jit(solution)/shard_map/while/body/eval_jaxpr/jit(_take)/select_n | solution.py:15
  301.7 11.9 %copy.23 = bf16[64,256,256]{1,2,0:T(8,128)(2,1)} copy(bf16[64,256,256]{2,1,0:T(8,128)(2,1)} %get-tuple-element.16) | data formatting | bytes 16777216 | tf_op jit(solution)/shard_map/while/body/eval_jaxpr/jit(_take)/select_n | solution.py:15
  313.7 7.5 %reshape.98 = bf16[4096,4,64]{2,1,0:T(4,128)(2,1)} reshape(bf16[16,2,32768]{2,1,0:T(2,128)(2,1)} %all-to-all-done.2) | data formatting | bytes 4194304
  321.1 5.4 %copy.25 = bf16[4,64,16,256]{3,1,0,2:T(8,128)(2,1)S(1)} copy(bf16[4,64,16,256]{1,0,3,2:T(4,128)(2,1)} %bitcast.87) | data formatting | bytes 4194304 | tf_op jit(solution)/shard_map/all_to_all | solution.py:55
  326.5 3.3 reshape.64
  329.7 11.9 %copy.22 = bf16[64,256,256]{1,2,0:T(8,128)(2,1)} copy(bf16[64,256,256]{2,1,0:T(8,128)(2,1)} %get-tuple-element.17) | data formatting | bytes 16777216 | tf_op jit(solution)/shard_map/while/body/eval_jaxpr/jit(_take)/select_n | solution.py:16
  341.7 12.7 %fusion.6 = f32[64,4,256,64]{2,3,1,0:T(8,128)} fusion(bf16[64,256,4,64]{1,3,2,0:T(8,128)(2,1)} %bitcast.82, bf16[64,64,4,64]{3,2,1,0:T(4,128)(2,1)} %reshape.64), kind=kOutput, calls=%fused_computation.11 | convolution fusion | flops 536870912 | bytes 27262976 | tf_op jit(solution)/shard_map/while/body/eval_jaxpr/tihd,tjhd->thij/dot_general | solution.py:18
  354.4 14.5 %fusion.18 = f32[64,4,64]{2,1,0:T(4,128)S(1)} fusion(f32[64,4,256,64]{2,3,1,0:T(8,128)} %fusion.6), kind=kOutput, calls=%fused_computation.41 | output fusion | flops 8388863 | bytes 16842752 | tf_op jit(solution)/shard_map/while/body/eval_jaxpr/sub | solution.py:22
  368.9 43.2 %fusion.8 = bf16[64,4,64,64]{3,2,1,0:T(8,128)(2,1)} fusion(bf16[64,256,4,64]{1,3,2,0:T(8,128)(2,1)} %bitcast.91, f32[64,4,64]{2,1,0:T(4,128)S(1)} %fusion.18, f32[64,4,256,64]{2,3,1,0:T(8,128)} %fusion.6), kind=kOutput, calls=%fused_computation.13 | convolution fusion | flops 550519040 | bytes 27328512 | tf_op jit(solution)/shard_map/while/body/eval_jaxpr/thij,tjhd->tihd/dot_general | solution.py:24
  412.1 4.8 copy.27
  416.9 7.7 %all-to-all-start.3 = ((bf16[64,64,256]{2,1,0:T(8,128)(2,1)}), bf16[64,64,256]{2,1,0:T(8,128)(2,1)S(1)}, u32[]{:S(2)}, u32[]{:S(2)}) async-start(bf16[64,64,256]{2,1,0:T(8,128)(2,1)} %copy.27), calls=%async_computation.3 | async-start | bytes 4194304 | tf_op jit(solution)/shard_map/all_to_all | solution.py:57
  424.7 47.3 %all-to-all-done.3 = bf16[64,64,256]{2,1,0:T(8,128)(2,1)S(1)} async-done(((bf16[64,64,256]{2,1,0:T(8,128)(2,1)}), bf16[64,64,256]{2,1,0:T(8,128)(2,1)S(1)}, u32[]{:S(2)}, u32[]{:S(2)}) %all-to-all-start.3) | async-done | bytes 2097184 | tf_op jit(solution)/shard_map/all_to_all | solution.py:57
  474.1 9.3 %convolution_convert_fusion = bf16[256,2048]{1,0:T(8,128)(2,1)} fusion(bf16[4096,2048]{1,0:T(8,128)(2,1)} %all-gather.3.cloned.1.call-done, bf16[256,4096]{1,0:T(8,128)(2,1)S(1)} %bitcast.95, pred[256]{0:T(512)(128)(4,1)S(1)} %lt.30), kind=kOutput, calls=%fused_computation.14 | convolution fusion | flops 4296540160 | bytes 19923200 | tf_op jit(solution)/shard_map/dot_general | solution.py:63
  (36 shorter events, 14.7 us)
Async XLA Ops:
  6.5 8.5 %copy-start = (bf16[1,256,4096]{2,1,0:T(8,128)(2,1)S(1)}, bf16[1,256,4096]{2,1,0:T(8,128)(2,1)}, u32[]{:S(2)}) copy-start(bf16[1,256,4096]{2,1,0:T(8,128)(2,1)} %param.9) | copy-start | bytes 6291460
  6.5 467.6 %all-gather.3.cloned.1.call-start = ((), (), s32[]{:S(2)}) async-start(), calls=%async_computation.4 | async-start | bytes 17825792 | tf_op jit(solution)/shard_map/all_gather | solution.py:65
  22.4 87.2 %all-to-all-start.1 = ((bf16[16,1,256,256]{3,2,1,0:T(8,128)(2,1)}), bf16[16,1,256,256]{3,2,1,0:T(8,128)(2,1)S(1)}, u32[]{:S(2)}, u32[]{:S(2)}) async-start(bf16[16,1,256,256]{3,2,1,0:T(8,128)(2,1)} %bitcast_dynamic-update-slice_fusion), calls=%async_computation.1 | async-start | bytes 4194304 | tf_op jit(solution)/shard_map/all_to_all | solution.py:48
  109.6 99.5 %all-to-all-start = ((bf16[16,2,32768]{2,1,0:T(2,128)(2,1)}), bf16[16,2,32768]{2,1,0:T(2,128)(2,1)}, u32[]{:S(2)}, u32[]{:S(2)}) async-start(bf16[16,2,32768]{2,1,0:T(2,128)(2,1)} %reshape.95), calls=%async_computation | async-start | bytes 4194304 | tf_op jit(solution)/shard_map/all_to_all | solution.py:53
  128.4 85.4 %copy-start.3 = (u32[32]{0:T(128)S(1)}, u32[32]{0:T(128)}, u32[]{:S(2)}) copy-start(u32[32]{0:T(128)} %constant.37) | copy-start | bytes 388
  128.4 86.7 %copy-start.1 = (s32[4,1]{0,1:T(1,128)S(1)}, s32[4,1]{0,1:T(1,128)}, u32[]{:S(2)}) copy-start(s32[4,1]{0,1:T(1,128)} %param.12) | copy-start | bytes 52
  209.1 104.5 %all-to-all-start.2 = ((bf16[16,2,32768]{2,1,0:T(2,128)(2,1)}), bf16[16,2,32768]{2,1,0:T(2,128)(2,1)}, u32[]{:S(2)}, u32[]{:S(2)}) async-start(bf16[16,2,32768]{2,1,0:T(2,128)(2,1)} %reshape.97), calls=%async_computation.2 | async-start | bytes 4194304 | tf_op jit(solution)/shard_map/all_to_all | solution.py:55
  416.9 7.7 %copy-start.2 = (s32[4]{0:T(128)S(1)}, s32[4]{0:T(128)}, u32[]{:S(2)}) copy-start(s32[4]{0:T(128)} %param.13) | copy-start | bytes 52
  416.9 55.1 %all-to-all-start.3 = ((bf16[64,64,256]{2,1,0:T(8,128)(2,1)}), bf16[64,64,256]{2,1,0:T(8,128)(2,1)S(1)}, u32[]{:S(2)}, u32[]{:S(2)}) async-start(bf16[64,64,256]{2,1,0:T(8,128)(2,1)} %copy.27), calls=%async_computation.3 | async-start | bytes 4194304 | tf_op jit(solution)/shard_map/all_to_all | solution.py:57
Sparse Core Ops, SparseCore 0:
  9.5 202.2 all-gather.2
